TPU v7x, 32 devices: a whole 2x2x4 slice. The times are simulated.
32 devices in a mesh: blk: 8 (over z, x), mp: 4 (over y, core).
Axes of the slice: x: 2, y: 2, z: 4, core: 2. Of those that a mesh axis runs over, the one named last changes fastest.
Arguments:
- tokens_in: bfloat16 [2048, 2048], P('blk'), may hold values from -17 to 17
- w_qkv: bfloat16 [3, 2048, 2048], P(None, None, 'mp'), may hold values from -0.125 to 0.125
- w_out: bfloat16 [2048, 2048], P('mp'), may hold values from -0.125 to 0.125
- grad_y: bfloat16 [2048, 2048], P('blk'), may hold values from -6 to 6
- block_cols: int32 [16, 2], replicated, may hold values from 0 to 15, as said below
- block_count: int32 [16], replicated, may hold values from 1 to 2, as said below
Outputs:
- grad_x: bfloat16 [2048, 2048], P('blk', 'mp')
- grad_qkv: bfloat16 [3, 2048, 2048], P(None, 'blk', 'mp')
- grad_out: bfloat16 [2048, 2048], P('mp', 'blk')
Inputs may be any that keep to these rules, and one draw needn't show every extreme that they name: `block_cols`: slot 0 of row r is r itself; the first block_count[r] slots of a row are distinct blocks; later slots repeat r. `block_count`: some rows use all 2 slots.
All inputs are finite; a program needn't handle non-finite values.
Results may differ from a plain program's by a relative error of at most 0.02.
Values may be sent and summed in bfloat16 or wider, within the bound.
No kernel may reach another device: no remote copies, remote signals or barrier semaphores. Data moves between devices by JAX's collectives and lax.ppermute only.
A program may use at most 64 MiB of HBM per device.

v0:
```python
import math
import jax
import jax.numpy as jnp
from jax import lax
from jax.sharding import PartitionSpec as P

HEAD = 128
BLOCK = 128
NEG_FILL = -1e30


def local(tokens_in, w_qkv, w_out, grad_y, block_cols, block_count):
    tok_rows = tokens_in.shape[0]
    heads_dev = w_out.shape[0] // HEAD
    local_blocks = tok_rows // BLOCK
    block_total = block_cols.shape[0]
    slot_total = block_cols.shape[1]
    score_scale = 1.0 / math.sqrt(HEAD)
    projected = jnp.einsum(
        "td,cde->cte", tokens_in, w_qkv, preferred_element_type=jnp.float32
    ).astype(jnp.bfloat16)
    heads_view = projected.reshape(3, tok_rows, heads_dev, HEAD)
    queries, keys_loc, values_loc = (heads_view[0], heads_view[1], heads_view[2])
    keys_all, values_all = (
        lax.all_gather(keys_loc, "blk", axis=0, tiled=True),
        lax.all_gather(values_loc, "blk", axis=0, tiled=True),
    )
    key_blocks = keys_all.reshape(block_total, BLOCK, heads_dev, HEAD)
    value_blocks = values_all.reshape(block_total, BLOCK, heads_dev, HEAD)
    row_ids = lax.axis_index("blk") * local_blocks + jnp.arange(local_blocks, dtype=jnp.int32)
    my_cols = jnp.take(block_cols, row_ids, axis=0)
    my_counts = jnp.take(block_count, row_ids, axis=0)
    q_blocks = queries.reshape(local_blocks, BLOCK, heads_dev, HEAD)

    def slot_operands(slot):
        col_ids = lax.dynamic_index_in_dim(my_cols, slot, 1, keepdims=False)
        live_rows = slot < my_counts
        k_part = jnp.take(key_blocks, col_ids, axis=0)
        v_part = jnp.take(value_blocks, col_ids, axis=0)
        raw_scores = (
            jnp.einsum("bqhe,bkhe->bhqk", q_blocks, k_part, preferred_element_type=jnp.float32)
            * score_scale
        )
        return (col_ids, live_rows, k_part, v_part, raw_scores)

    def stats_slot(slot, carried):
        run_max, run_sum = carried
        col_ids, live_rows, k_part, v_part, raw_scores = slot_operands(slot)
        live_wide = live_rows[:, None, None, None]
        masked = jnp.where(live_wide, raw_scores, NEG_FILL)
        new_max = jnp.maximum(run_max, jnp.max(masked, axis=3))
        exps = jnp.where(live_wide, jnp.exp(masked - new_max[..., None]), 0.0)
        run_sum = run_sum * jnp.exp(run_max - new_max) + jnp.sum(exps, axis=3)
        return (new_max, run_sum)

    start_max = jnp.full((local_blocks, heads_dev, BLOCK), NEG_FILL, jnp.float32)
    start_sum = jnp.zeros((local_blocks, heads_dev, BLOCK), jnp.float32)
    run_max, run_sum = lax.fori_loop(0, slot_total, stats_slot, (start_max, start_sum))
    log_sum = run_max + jnp.log(run_sum)

    def value_slot(slot, accumulated):
        col_ids, live_rows, k_part, v_part, raw_scores = slot_operands(slot)
        live_wide = live_rows[:, None, None, None]
        weights = jnp.where(live_wide, jnp.exp(raw_scores - log_sum[..., None]), 0.0).astype(
            jnp.bfloat16
        )
        return accumulated + jnp.einsum(
            "bhqk,bkhe->bhqe", weights, v_part, preferred_element_type=jnp.float32
        )

    start_acc = jnp.zeros((local_blocks, heads_dev, BLOCK, HEAD), jnp.float32)
    accumulated = lax.fori_loop(0, slot_total, value_slot, start_acc)
    attended_blk = accumulated.astype(jnp.bfloat16)
    attended = attended_blk.transpose(0, 2, 1, 3).reshape(tok_rows, heads_dev, HEAD)
    o_flat = attended.reshape(tok_rows, heads_dev * HEAD)
    grad_heads = (
        jnp.dot(grad_y, w_out.T, preferred_element_type=jnp.float32)
        .astype(jnp.bfloat16)
        .reshape(tok_rows, heads_dev, HEAD)
    )
    g_blocks = grad_heads.reshape(local_blocks, BLOCK, heads_dev, HEAD)
    delta_blk = jnp.einsum(
        "bhqe,bqhe->bhq", attended_blk.astype(jnp.float32), g_blocks.astype(jnp.float32)
    )
    block_range = jnp.arange(block_total, dtype=jnp.int32)

    def backward_slot(slot, carried):
        col_ids, live_rows, k_part, v_part, raw_scores = slot_operands(slot)
        live_wide = live_rows[:, None, None, None]
        prob_rows = jnp.where(live_wide, jnp.exp(raw_scores - log_sum[..., None]), 0.0)
        dprobs = jnp.einsum("bqhe,bkhe->bhqk", g_blocks, v_part, preferred_element_type=jnp.float32)
        dscores = (prob_rows * (dprobs - delta_blk[..., None])).astype(jnp.bfloat16)
        dq_acc = carried[0] + jnp.einsum(
            "bhqk,bkhe->bqhe", dscores, k_part, preferred_element_type=jnp.float32
        )
        owner = ((col_ids[:, None] == block_range[None, :]) & live_rows[:, None]).astype(
            jnp.float32
        )
        dk_term = (
            jnp.einsum("bhqk,bqhe->bkhe", dscores, q_blocks, preferred_element_type=jnp.float32)
            * score_scale
        )
        dv_term = jnp.einsum(
            "bhqk,bqhe->bkhe",
            prob_rows.astype(jnp.bfloat16),
            g_blocks,
            preferred_element_type=jnp.float32,
        )
        dk_full = carried[1] + jnp.einsum(
            "bn,bkhe->nkhe", owner, dk_term, precision=lax.Precision.HIGHEST
        )
        dv_full = carried[2] + jnp.einsum(
            "bn,bkhe->nkhe", owner, dv_term, precision=lax.Precision.HIGHEST
        )
        return (dq_acc, dk_full, dv_full)

    dq_start = jnp.zeros((local_blocks, BLOCK, heads_dev, HEAD), jnp.float32)
    full_zero = jnp.zeros((block_total, BLOCK, heads_dev, HEAD), jnp.float32)
    back_start = (dq_start, full_zero, full_zero)
    back_out = lax.fori_loop(0, slot_total, backward_slot, back_start)
    grad_q = (back_out[0] * score_scale).astype(jnp.bfloat16).reshape(tok_rows, heads_dev, HEAD)
    stacked = jnp.stack(
        [
            back_out[1].reshape(block_total * BLOCK, heads_dev, HEAD),
            back_out[2].reshape(block_total * BLOCK, heads_dev, HEAD),
        ],
        axis=1,
    )
    key_grads = lax.psum_scatter(stacked, "blk", scatter_dimension=0, tiled=True)
    grad_k = key_grads[:, 0].astype(jnp.bfloat16)
    grad_v = key_grads[:, 1].astype(jnp.bfloat16)
    grads_stack = jnp.stack([grad_q, grad_k, grad_v]).reshape(3, tok_rows, heads_dev * HEAD)
    dx_term = jnp.einsum("cte,cde->td", grads_stack, w_qkv, preferred_element_type=jnp.float32)
    grad_x = lax.psum_scatter(dx_term, "mp", scatter_dimension=1, tiled=True).astype(jnp.bfloat16)
    qkv_term = jnp.einsum("td,cte->cde", tokens_in, grads_stack, preferred_element_type=jnp.float32)
    out_term = jnp.dot(o_flat.T, grad_y, preferred_element_type=jnp.float32)
    grad_qkv, grad_out = (
        lax.psum_scatter(qkv_term, "blk", scatter_dimension=1, tiled=True),
        lax.psum_scatter(out_term, "blk", scatter_dimension=1, tiled=True),
    )
    return (grad_x, grad_qkv.astype(jnp.bfloat16), grad_out.astype(jnp.bfloat16))


def solution(mesh):
    in_specs = (P("blk", None), P(None, None, "mp"), P("mp", None), P("blk", None), P(), P())
    out_specs = (P("blk", "mp"), P(None, "blk", "mp"), P("mp", "blk"))
    return jax.shard_map(local, mesh=mesh, in_specs=in_specs, out_specs=out_specs, check_vma=False)
```

profile of v0, /device:TPU:0, one launch (start us, length us, event | category | flops | bytes accessed | tf_op | source)
XLA Modules:
  0.0 675.0 jit_solution(446797628690224736)
XLA Ops:
  7.2 5.0 fusion.40
  12.3 0.8 fusion.48
  13.2 0.7 all-gather.5.cloned.1.call-update
  14.1 0.6 gather_fusion.5
  15.2 0.6 gather_fusion.6
  16.0 2.0 convolution_convert_fusion.1
  18.1 49.0 %all-gather.3.cloned.1.call-done = bf16[2048,4,128]{0,2,1:T(8,128)(2,1)} async-done(((bf16[256,4,128]{0,2,1:T(8,128)(2,1)}), bf16[2048,4,128]{0,2,1:T(8,128)(2,1)}) %all-gather.3.cloned.1.call-update) | async-done | bytes 2097168 | tf_op jit(solution)/shard_map/all_gather | solution.py:25
  67.1 4.3 copy.39
  71.4 6.3 while.48
  71.4 2.4 gather_fusion
  74.0 0.3 fusion.92
  74.6 2.5 gather_fusion
  77.2 0.3 fusion.92
  77.7 41.2 %all-gather.5.cloned.1.call-done = bf16[2048,4,128]{0,2,1:T(8,128)(2,1)} async-done(((bf16[256,4,128]{0,2,1:T(8,128)(2,1)}), bf16[2048,4,128]{0,2,1:T(8,128)(2,1)}) %all-gather.5.cloned.1.call-update) | async-done | bytes 2097168 | tf_op jit(solution)/shard_map/all_gather | solution.py:26
  119.0 4.3 copy.42
  123.3 11.2 %while.49 = (s32[]{:T(128)}, f32[2,4,128,128]{3,2,1,0:T(8,128)S(1)}, s32[2]{0:T(128)S(1)}, s32[2,2]{0,1:T(2,128)S(1)}, bf16[16,128,4,128]{3,2,1,0:T(4,128)(2,1)}...) while((s32[]{:T(128)}, ...), condition=%wide.region_5.7_spmd.clone, body=%wide.region_4.6_spmd.clone.sunk | while | flops 68158480 | bytes 3941551 | solution.py:72
  123.3 2.4 gather_fusion.2
  125.7 2.4 gather_fusion.1
  128.1 0.3 broadcast_select_fusion.11
  128.4 0.5 convolution_add_fusion.2
  128.9 2.4 gather_fusion.2
  131.3 2.4 gather_fusion.1
  133.7 0.3 broadcast_select_fusion.11
  134.0 0.5 convolution_add_fusion.2
  134.5 0.8 copy-done.11
  135.3 1.1 convert_bitcast_fusion
  136.4 0.5 multiply_reduce_fusion
  137.0 33.5 %while.50 = (s32[]{:T(128)}, f32[2,128,4,128]{1,3,2,0:T(8,128)S(1)}, f32[16,128,4,128]{3,0,2,1:T(8,128)}, f32[16,128,4,128]{3,0,2,1:T(8,128)}, s32[2,2]{0,1:T(2,...) while((s32[]{:T(128)}, ...), condition=%wide.region_7.9_spmd.clone, body=%wide.region_6.8_spmd.clone.sunk | while | flops 223872144 | bytes 93861216 | solution.py:120
  137.2 2.4 gather_fusion.4
  139.6 2.4 gather_fusion.3
  141.9 0.3 broadcast_select_fusion.12
  142.4 0.3 fusion.111
  142.8 0.3 fusion.112
  143.3 0.3 fusion.113
  143.8 0.8 copy-done.5
  144.6 3.6 select_add_fusion.4
  148.2 3.6 select_add_fusion.5
  151.8 2.0 copy-done.4
  153.8 2.4 gather_fusion.4
  156.2 2.4 gather_fusion.3
  158.6 0.3 broadcast_select_fusion.12
  159.1 0.3 fusion.111
  159.4 0.3 fusion.112
  160.0 0.3 fusion.113
  160.5 0.8 copy-done.5
  161.3 3.6 select_add_fusion.4
  164.9 3.6 select_add_fusion.5
  168.5 2.0 copy-done.4
  170.4 4.8 copy.50
  175.2 2.4 copy.49
  177.7 3.8 pad_maximum_fusion
  181.7 0.9 copy-done.9
  182.7 2.7 fusion.43
  185.8 143.0 %reduce-scatter.5.cloned.1.call-done = f32[256,2,4,128]{3,0,2,1:T(8,128)} async-done(((f32[2048,2,4,128]{3,0,2,1:T(8,128)}), f32[256,2,4,128]{3,0,2,1:T(8,128)}) %reduce-scatter.5.cloned.1.call-update) | async-done | bytes 1048592 | tf_op jit(solution)/shard_map/reduce_scatter | solution.py:129
  328.8 1.3 convert.7
  330.9 6.0 convolution_bitcast_fusion.2
  337.0 6.4 convolution_bitcast_fusion.1
  343.4 76.8 %reduce-scatter.11.cloned.1.call-done = f32[512,256]{1,0:T(8,128)} async-done(((f32[512,2048]{1,0:T(8,128)}), f32[512,256]{1,0:T(8,128)}) %reduce-scatter.11.cloned.1.call-update) | async-done | bytes 524304 | tf_op jit(solution)/shard_map/reduce_scatter | solution.py:139
  420.3 1.8 convert_element_type.81
  422.0 31.9 %reduce-scatter.7.cloned.1.call-done = f32[256,512]{1,0:T(8,128)} async-done(((f32[256,2048]{1,0:T(8,128)}), f32[256,512]{1,0:T(8,128)}) %reduce-scatter.7.cloned.1.call-update) | async-done | bytes 524304 | tf_op jit(solution)/shard_map/reduce_scatter | solution.py:134
  453.9 1.8 convert_element_type.79
  455.7 209.9 %reduce-scatter.9.cloned.1.call-done = f32[3,256,512]{1,2,0:T(8,128)} async-done(((f32[3,2048,512]{1,2,0:T(8,128)}), f32[3,256,512]{1,2,0:T(8,128)}) %reduce-scatter.9.cloned.1.call-update) | async-done | bytes 1572880 | tf_op jit(solution)/shard_map/reduce_scatter | solution.py:138
  665.5 1.5 convert_element_type.80
  667.0 1.2 copy.55
  (101 shorter events, 4.7 us)
Async XLA Ops:
  7.2 8.8 %copy-start = (bf16[512,2048]{1,0:T(8,128)(2,1)S(1)}, bf16[512,2048]{1,0:T(8,128)(2,1)}, u32[]{:S(2)}) copy-start(bf16[512,2048]{1,0:T(8,128)(2,1)} %param.16) | copy-start | bytes 6291460
  7.2 6.8 %copy-start.12 = (s32[16,2]{0,1:T(2,128)S(1)}, s32[16,2]{0,1:T(2,128)}, u32[]{:S(2)}) copy-start(s32[16,2]{0,1:T(2,128)} %param.18) | copy-start | bytes 388
  7.2 8.0 %copy-start.2 = (s32[16]{0:T(128)S(1)}, s32[16]{0:T(128)}, u32[]{:S(2)}) copy-start(s32[16]{0:T(128)} %param.19) | copy-start | bytes 196
  7.2 59.9 %all-gather.3.cloned.1.call-start = ((), (), s32[]{:S(2)}) async-start(), calls=%async_computation.4 | async-start | bytes 2359296 | tf_op jit(solution)/shard_map/all_gather | solution.py:25
  13.1 105.8 %all-gather.5.cloned.1.call-start = ((), (), s32[]{:S(2)}) async-start(), calls=%async_computation.5 | async-start | bytes 2359296 | tf_op jit(solution)/shard_map/all_gather | solution.py:26
  13.9 314.9 %reduce-scatter.5.cloned.1.call-start = ((), (), s32[]{:S(2)}) async-start(), calls=%async_computation.6 | async-start | bytes 9437184 | tf_op jit(solution)/shard_map/reduce_scatter | solution.py:129
  77.7 45.6 %copy-start.10 = (f32[2,4,128,128]{3,2,1,0:T(8,128)S(1)}, f32[2,4,128,128]{3,2,1,0:T(8,128)}, u32[]{:S(2)}) copy-start(f32[2,4,128,128]{3,2,1,0:T(8,128)} %custom-call.2) | copy-start | bytes 1572868
  134.5 0.8 copy-start.11
  142.4 2.2 copy-start.5
  144.6 3.6 copy-start.3
  148.2 3.6 copy-start.6
  151.8 2.0 copy-start.4
  159.1 2.2 copy-start.5
  161.3 3.6 copy-start.3
  164.9 3.6 copy-start.6
  168.4 2.0 copy-start.4
  170.4 4.8 copy-start.7
  181.5 1.2 copy-start.9
  181.5 238.8 %reduce-scatter.11.cloned.1.call-start = ((), (), s32[]{:S(2)}) async-start(), calls=%async_computation.9 | async-start | bytes 4718592 | tf_op jit(solution)/shard_map/reduce_scatter | solution.py:139
  185.4 268.5 %reduce-scatter.7.cloned.1.call-start = ((), (), s32[]{:S(2)}) async-start(), calls=%async_computation.7 | async-start | bytes 2621440 | tf_op jit(solution)/shard_map/reduce_scatter | solution.py:134
  330.9 6.1 copy-start.8
  337.0 328.6 %reduce-scatter.9.cloned.1.call-start = ((), (), s32[]{:S(2)}) async-start(), calls=%async_computation.8 | async-start | bytes 14155776 | tf_op jit(solution)/shard_map/reduce_scatter | solution.py:138
  343.4 324.8 %copy-start.1 = (bf16[512,2048]{1,0:T(8,128)(2,1)S(1)}, bf16[512,2048]{1,0:T(8,128)(2,1)}, u32[]{:S(2)}) copy-start(bf16[512,2048]{1,0:T(8,128)(2,1)} %param.16) | copy-start | bytes 6291460
Sparse Core Ops, SparseCore 0:
  13.3 53.7 all-gather.2
  69.7 49.2 all-gather.4
  181.6 147.1 reduce-scatter.4
  332.8 87.4 reduce-scatter.10
  422.6 31.2 reduce-scatter.6
  457.8 207.7 reduce-scatter.8
where the time goes:
time: 676 us; the launch traced here: 675 us
  waiting for transfers between devices  553 us (82%)
  local copies, waits for them, and re-layouts  52.7 us (8%)
  matrix products  40.6 us (6%)
  between operations  14.4 us (2%)
  other arithmetic  13.8 us (2%)
    reduce_scatter x1, waiting for transfers between devices, local(): lax.psum_scatter(qkv_term, 'blk', scatter_dimension=1, tiled=True)  210 us
    reduce_scatter x1, waiting for transfers between devices, local(): lax.psum_scatter(stacked, 'blk', scatter_dimension=0, tiled=True)  143 us
    reduce_scatter x1, waiting for transfers between devices, local(): lax.psum_scatter(out_term, 'blk', scatter_dimension=1, tiled=True)  76.8 us
    all_gather x1, waiting for transfers between devices, local(): lax.all_gather(keys_loc, 'blk', axis=0, tiled=True)  49 us
    all_gather x1, waiting for transfers between devices, local(): lax.all_gather(values_loc, 'blk', axis=0, tiled=True)  41.2 us
    reduce_scatter x1, waiting for transfers between devices, local(): lax.psum_scatter(dx_term, 'mp', scatter_dimension=1, tiled=True)  31.9 us
    gather x6, local copies, waits for them, and re-layouts, slot_operands(): k_part = jnp.take(key_blocks, col_ids, axis=0)  14.3 us
  transfers between devices with their start and end apart: 6, of which 6 were waited for; matrix products, arithmetic and copies ran while one was open for 5% of the time, Pallas kernels for 0%

commit v1 on v0

--- a/solution.py
+++ b/solution.py
@@ -10,6 +10,22 @@
 
 
 def local(tokens_in, w_qkv, w_out, grad_y, block_cols, block_count):
+
+    def group_write(own_rows, dim_k):
+        axis_name = "blk"
+        o_now, w_next = (lax.axis_size(axis_name), lax.axis_index(axis_name))
+        ready, far_arr = (own_rows, 1)
+        while far_arr < o_now:
+            frames = []
+            for q in range(o_now):
+                frames.append((q, q ^ far_arr))
+            back = lax.ppermute(ready, axis_name=axis_name, perm=frames)
+            found_now = jnp.concatenate([ready, back], axis=dim_k)
+            met_up = jnp.concatenate([back, ready], axis=dim_k)
+            ready = jnp.where(w_next & far_arr == 0, found_now, met_up)
+            far_arr = 2 * far_arr
+        return ready
+
     tok_rows = tokens_in.shape[0]
     heads_dev = w_out.shape[0] // HEAD
     local_blocks = tok_rows // BLOCK
@@ -23,7 +39,7 @@
     queries, keys_loc, values_loc = (heads_view[0], heads_view[1], heads_view[2])
     keys_all, values_all = (
         lax.all_gather(keys_loc, "blk", axis=0, tiled=True),
-        lax.all_gather(values_loc, "blk", axis=0, tiled=True),
+        group_write(values_loc, 0),
     )
     key_blocks = keys_all.reshape(block_total, BLOCK, heads_dev, HEAD)
     value_blocks = values_all.reshape(block_total, BLOCK, heads_dev, HEAD)

time: 676 us -> 687 us (1.016)
  other arithmetic: 13.8 us -> 22.4 us
  starting transfers between devices: 0.24 us -> 7.55 us
    ppermute x0 -> x3, waiting for transfers between devices: none -> 83.9 us  [group_write(): back = lax.ppermute(ready, axis_name=axis_name, perm=frames)]
    all_gather x1, waiting for transfers between devices: 49 us -> 0.01 us  [local(): lax.all_gather(keys_loc, 'blk', axis=0, tiled=True)]
    all_gather x1 -> x0, waiting for transfers between devices: 41.2 us -> none  [local(): lax.all_gather(values_loc, 'blk', axis=0, tiled=True)]
    select_n x0 -> x3, other arithmetic: none -> 8.52 us  [group_write(): ready = jnp.where(w_next & far_arr == 0, found_now, met_up)]
    ppermute x0 -> x3, starting transfers between devices: none -> 7.35 us  [group_write(): back = lax.ppermute(ready, axis_name=axis_name, perm=frames)]
  transfers between devices with their start and end apart: 6 -> 8, of which waited for: 6 -> 7; matrix products, arithmetic and copies ran while one was open for 5% -> 6% of each run, Pallas kernels for 0% -> 0%
where the time goes in v1:
time: 687 us; the launch traced here: 686 us
  waiting for transfers between devices  548 us (80%)
  local copies, waits for them, and re-layouts  52.6 us (8%)
  matrix products  40.6 us (6%)
  other arithmetic  22.4 us (3%)
  between operations  14.1 us (2%)
  starting transfers between devices  7.55 us (1%)
    reduce_scatter x1, waiting for transfers between devices, local(): lax.psum_scatter(qkv_term, 'blk', scatter_dimension=1, tiled=True)  210 us
    reduce_scatter x1, waiting for transfers between devices, local(): lax.psum_scatter(stacked, 'blk', scatter_dimension=0, tiled=True)  146 us
    ppermute x3, waiting for transfers between devices, group_write(): back = lax.ppermute(ready, axis_name=axis_name, perm=frames)  83.9 us
    reduce_scatter x1, waiting for transfers between devices, local(): lax.psum_scatter(out_term, 'blk', scatter_dimension=1, tiled=True)  77 us
    reduce_scatter x1, waiting for transfers between devices, local(): lax.psum_scatter(dx_term, 'mp', scatter_dimension=1, tiled=True)  31.8 us
    gather x6, local copies, waits for them, and re-layouts, slot_operands(): k_part = jnp.take(key_blocks, col_ids, axis=0)  14.3 us
  transfers between devices with their start and end apart: 8, of which 7 were waited for; matrix products, arithmetic and copies ran while one was open for 6% of the time, Pallas kernels for 0%

profile of v1, /device:TPU:0, one launch (start us, length us, event | category | flops | bytes accessed | tf_op | source)
XLA Modules:
  0.0 686.2 jit_solution(13511253557558873381)
XLA Ops:
  7.2 5.0 fusion.40
  12.3 0.8 fusion.48
  13.1 3.0 collective-permute-start
  16.1 6.3 collective-permute-done
  22.4 0.9 maximum_select_fusion.2
  23.4 1.8 collective-permute-start.1
  25.8 19.4 %collective-permute-done.1 = bf16[512,4,128]{0,2,1:T(8,128)(2,1)} collective-permute-done((bf16[512,4,128]{0,2,1:T(8,128)(2,1)}, bf16[512,4,128]{0,2,1:T(8,128)(2,1)}, u32[]{:S(2)}, u32[]{:S(2)}) %collective-permute-start.1) | collective-permute-done | bytes 524320 | tf_op jit(solution)/shard_map/ppermute | solution.py:22
  45.2 3.0 maximum_select_fusion.1
  48.2 2.5 collective-permute-start.2
  50.7 0.6 gather_fusion.6
  51.4 0.6 gather_fusion.5
  52.1 2.0 convolution_convert_fusion.1
  54.2 58.2 %collective-permute-done.2 = bf16[1024,4,128]{0,2,1:T(8,128)(2,1)} collective-permute-done((bf16[1024,4,128]{0,2,1:T(8,128)(2,1)}, bf16[1024,4,128]{0,2,1:T(8,128)(2,1)}, u32[]{:S(2)}, u32[]{:S(2)}) %collective-permute-start.2) | collective-permute-done | bytes 1048608 | tf_op jit(solution)/shard_map/ppermute | solution.py:22
  112.4 4.6 maximum_select_fusion
  117.0 4.3 copy.42
  121.3 4.3 copy.39
  125.6 6.3 while.48
  125.6 2.4 gather_fusion
  128.3 0.3 fusion.92
  128.8 2.4 gather_fusion
  131.4 0.3 fusion.92
  131.9 11.2 %while.49 = (s32[]{:T(128)}, f32[2,4,128,128]{3,2,1,0:T(8,128)S(1)}, s32[2]{0:T(128)S(1)}, s32[2,2]{0,1:T(2,128)S(1)}, bf16[16,128,4,128]{3,2,1,0:T(4,128)(2,1)}...) while((s32[]{:T(128)}, ...), condition=%wide.region_5.7_spmd.clone, body=%wide.region_4.6_spmd.clone.sunk | while | flops 68158480 | bytes 3941551 | solution.py:88
  131.9 2.4 gather_fusion.2
  134.3 2.4 gather_fusion.1
  137.0 0.5 convolution_add_fusion.2
  137.6 2.4 gather_fusion.2
  140.0 2.4 gather_fusion.1
  142.6 0.5 convolution_add_fusion.2
  143.2 0.8 copy-done.11
  143.9 1.1 convert_bitcast_fusion
  145.1 0.5 multiply_reduce_fusion
  145.6 33.5 %while.50 = (s32[]{:T(128)}, f32[2,128,4,128]{1,3,2,0:T(8,128)S(1)}, f32[16,128,4,128]{3,0,2,1:T(8,128)}, f32[16,128,4,128]{3,0,2,1:T(8,128)}, s32[2,2]{0,1:T(2,...) while((s32[]{:T(128)}, ...), condition=%wide.region_7.9_spmd.clone, body=%wide.region_6.8_spmd.clone.sunk | while | flops 223872144 | bytes 93861216 | solution.py:136
  145.8 2.4 gather_fusion.4
  148.2 2.4 gather_fusion.3
  151.1 0.3 fusion.111
  151.4 0.3 fusion.112
  152.5 0.8 copy-done.5
  153.3 3.6 select_add_fusion.4
  156.9 3.6 select_add_fusion.5
  160.4 2.0 copy-done.4
  162.5 2.4 gather_fusion.4
  164.9 2.4 gather_fusion.3
  167.7 0.3 fusion.111
  168.1 0.3 fusion.112
  169.1 0.8 copy-done.5
  169.9 3.6 select_add_fusion.4
  173.5 3.6 select_add_fusion.5
  177.1 2.0 copy-done.4
  179.1 4.8 copy.50
  183.9 2.4 copy.49
  186.3 3.8 pad_maximum_fusion
  190.4 0.9 copy-done.9
  191.3 2.7 fusion.43
  194.5 145.7 %reduce-scatter.5.cloned.1.call-done = f32[256,2,4,128]{3,0,2,1:T(8,128)} async-done(((f32[2048,2,4,128]{3,0,2,1:T(8,128)}), f32[256,2,4,128]{3,0,2,1:T(8,128)}) %reduce-scatter.5.cloned.1.call-update) | async-done | bytes 1048592 | tf_op jit(solution)/shard_map/reduce_scatter | solution.py:145
  340.2 1.3 convert.7
  342.3 6.0 convolution_bitcast_fusion.2
  348.4 6.4 convolution_bitcast_fusion.1
  354.8 77.0 %reduce-scatter.11.cloned.1.call-done = f32[512,256]{1,0:T(8,128)} async-done(((f32[512,2048]{1,0:T(8,128)}), f32[512,256]{1,0:T(8,128)}) %reduce-scatter.11.cloned.1.call-update) | async-done | bytes 524304 | tf_op jit(solution)/shard_map/reduce_scatter | solution.py:155
  431.7 1.8 convert_element_type.81
  433.5 31.8 %reduce-scatter.7.cloned.1.call-done = f32[256,512]{1,0:T(8,128)} async-done(((f32[256,2048]{1,0:T(8,128)}), f32[256,512]{1,0:T(8,128)}) %reduce-scatter.7.cloned.1.call-update) | async-done | bytes 524304 | tf_op jit(solution)/shard_map/reduce_scatter | solution.py:150
  465.3 1.8 convert_element_type.79
  467.1 209.9 %reduce-scatter.9.cloned.1.call-done = f32[3,256,512]{1,2,0:T(8,128)} async-done(((f32[3,2048,512]{1,2,0:T(8,128)}), f32[3,256,512]{1,2,0:T(8,128)}) %reduce-scatter.9.cloned.1.call-update) | async-done | bytes 1572880 | tf_op jit(solution)/shard_map/reduce_scatter | solution.py:154
  677.0 1.5 convert_element_type.80
  678.5 1.2 copy.55
  (107 shorter events, 6.3 us)
Async XLA Ops:
  7.2 44.9 %copy-start = (bf16[512,2048]{1,0:T(8,128)(2,1)S(1)}, bf16[512,2048]{1,0:T(8,128)(2,1)}, u32[]{:S(2)}) copy-start(bf16[512,2048]{1,0:T(8,128)(2,1)} %param.16) | copy-start | bytes 6291460
  7.2 114.1 %all-gather.2.cloned.1.call-start = ((), (), s32[]{:S(2)}) async-start(), calls=%async_computation.4 | async-start | bytes 2359296 | tf_op jit(solution)/shard_map/all_gather | solution.py:41
  12.3 13.5 %copy-start.12 = (s32[16,2]{0,1:T(2,128)S(1)}, s32[16,2]{0,1:T(2,128)}, u32[]{:S(2)}) copy-start(s32[16,2]{0,1:T(2,128)} %param.18) | copy-start | bytes 388
  12.3 38.4 %copy-start.2 = (s32[16]{0:T(128)S(1)}, s32[16]{0:T(128)}, u32[]{:S(2)}) copy-start(s32[16]{0:T(128)} %param.19) | copy-start | bytes 196
  13.1 327.1 %reduce-scatter.5.cloned.1.call-start = ((), (), s32[]{:S(2)}) async-start(), calls=%async_computation.5 | async-start | bytes 9437184 | tf_op jit(solution)/shard_map/reduce_scatter | solution.py:145
  13.1 9.3 %collective-permute-start = (bf16[256,4,128]{0,2,1:T(8,128)(2,1)S(1)}, bf16[256,4,128]{0,2,1:T(8,128)(2,1)S(1)}, u32[]{:S(2)}, u32[]{:S(2)}) collective-permute-start(bf16[256,4,128]{0,2,1:T(8,128)(2,1)S(1)} %bitcast.114), channel_id=1, source_target_pairs={{0,4},{4,0},{8,12},{12,8},{16,20},{20,16},{24,28},{28,24},{1,5},{5... | collective-permute-start | bytes 786440 | tf_op jit(solution)/shard_map/ppermute | solution.py:22
  23.4 21.9 %collective-permute-start.1 = (bf16[512,4,128]{0,2,1:T(8,128)(2,1)}, bf16[512,4,128]{0,2,1:T(8,128)(2,1)}, u32[]{:S(2)}, u32[]{:S(2)}) collective-permute-start(bf16[512,4,128]{0,2,1:T(8,128)(2,1)} %maximum_select_fusion.2), channel_id=1, source_target_pairs={{0,8},{4,12},{8,0},{12,4},{16,24},{20,28},{24,16},{28,20},{1,9},{5... | collective-permute-start | bytes 1572872 | tf_op jit(solution)/shard_map/ppermute | solution.py:22
  48.2 64.2 %collective-permute-start.2 = (bf16[1024,4,128]{0,2,1:T(8,128)(2,1)}, bf16[1024,4,128]{0,2,1:T(8,128)(2,1)}, u32[]{:S(2)}, u32[]{:S(2)}) collective-permute-start(bf16[1024,4,128]{0,2,1:T(8,128)(2,1)} %maximum_select_fusion.1), channel_id=1, source_target_pairs={{0,16},{4,20},{8,24},{12,28},{16,0},{20,4},{24,8},{28,12},{1,17},{... | collective-permute-start | bytes 3145736 | tf_op jit(solution)/shard_map/ppermute | solution.py:22
  125.6 6.3 copy-start.10
  143.2 0.8 copy-start.11
  151.1 2.2 copy-start.5
  153.3 3.6 copy-start.3
  156.9 3.6 copy-start.6
  160.4 2.0 copy-start.4
  167.7 2.2 copy-start.5
  169.9 3.6 copy-start.3
  173.5 3.6 copy-start.6
  177.1 2.0 copy-start.4
  179.1 4.8 copy-start.7
  190.1 1.2 copy-start.9
  190.1 241.6 %reduce-scatter.11.cloned.1.call-start = ((), (), s32[]{:S(2)}) async-start(), calls=%async_computation.8 | async-start | bytes 4718592 | tf_op jit(solution)/shard_map/reduce_scatter | solution.py:155
  194.0 271.3 %reduce-scatter.7.cloned.1.call-start = ((), (), s32[]{:S(2)}) async-start(), calls=%async_computation.6 | async-start | bytes 2621440 | tf_op jit(solution)/shard_map/reduce_scatter | solution.py:150
  342.3 6.1 copy-start.8
  348.3 328.7 %reduce-scatter.9.cloned.1.call-start = ((), (), s32[]{:S(2)}) async-start(), calls=%async_computation.7 | async-start | bytes 14155776 | tf_op jit(solution)/shard_map/reduce_scatter | solution.py:154
  354.8 324.9 %copy-start.1 = (bf16[512,2048]{1,0:T(8,128)(2,1)S(1)}, bf16[512,2048]{1,0:T(8,128)(2,1)}, u32[]{:S(2)}) copy-start(bf16[512,2048]{1,0:T(8,128)(2,1)} %param.16) | copy-start | bytes 6291460
Sparse Core Ops, SparseCore 0:
  13.2 87.1 all-gather.1
  190.3 149.8 reduce-scatter.4
  344.3 87.4 reduce-scatter.10
  434.1 31.1 reduce-scatter.6
  469.2 207.7 reduce-scatter.8
